TPU v7x, 512 devices: a whole 4x8x8 slice. The times are simulated.
512 devices in a mesh: layer: 16 (over y, z_lo), blk: 32 (over z_hi, x, core).
Axes of the slice: x: 4, y: 8, z: 8 (z_hi: 4, z_lo: 2; z = z_hi * 2 + z_lo), core: 2. Of those that a mesh axis runs over, the one named last changes fastest.
Arguments:
- query_pool: bfloat16 [16, 256, 4096], P('layer', None, 'blk'), may hold values from -6 to 6
- query_ids: int32 [64], replicated, may hold values from 0 to 255
- eigenbasis: bfloat16 [16, 4096, 4096], P('layer', None, 'blk'), may hold values from -0.09375 to 0.09375
- eigenvalues: float32 [16, 4096], P('layer', 'blk'), may hold values from 0.003 to 30, as said below
- train_grads: bfloat16 [16, 8192, 4096], P('layer', 'blk'), may hold values from -0.008972168 to 0.008972168
- train_ids: int32 [8192], P('blk'), may hold values from 0 to 8191, as said below
Outputs:
- influence: float32 [64, 8192], P(None, 'blk')
Inputs may be any that keep to these rules, and one draw needn't show every extreme that they name: train_ids is a permutation of the example ids; the ids of one device's shard of 256 rows fall in equal numbers, 8 each, into every range of 256 consecutive ids starting at a multiple of 256. `eigenvalues`: positive.
All inputs are finite; a program needn't handle non-finite values.
Results may differ from a plain program's by a relative error of at most 0.0038.
Values may be sent and summed in bfloat16 or wider, within the bound.
A program may use at most 64 MiB of HBM per device.

v0:
```python
import jax
import jax.numpy as jnp
from jax import lax
from jax.sharding import PartitionSpec as P

WIDTH = 4096


def place_columns(arrived, slot_code):
    slot_pos = slot_code[0].astype(jnp.int32)
    inverse = jnp.argsort(slot_pos, stable=True)
    return jnp.take(arrived, inverse, axis=1)


def on_device(query_pool, query_ids, eigenbasis, eigenvalues, train_grads, train_ids):
    query_block = query_pool[0]
    eigen_cols = eigenbasis[0]
    eigen_vals = eigenvalues[0]
    train_rows = train_grads[0]
    local_train = train_rows.shape[0]
    selected = jnp.take(query_block, query_ids, axis=0)
    eigen_sum = lax.psum(jnp.sum(eigen_vals), "blk")
    damping = 0.1 * eigen_sum / WIDTH
    rotated = jnp.dot(
        lax.all_gather(selected, "blk", axis=1, tiled=True),
        eigen_cols,
        preferred_element_type=jnp.float32,
    )
    damped = (rotated / (eigen_vals + damping)).astype(jnp.bfloat16)
    partial_terms = lax.dot_general(
        damped, eigen_cols, (((1,), (1,)), ((), ())), preferred_element_type=jnp.float32
    )
    precond = lax.psum(partial_terms, "blk").astype(jnp.bfloat16)
    scores = lax.dot_general(
        precond, train_rows, (((1,), (1,)), ((), ())), preferred_element_type=jnp.float32
    )
    owner = train_ids // local_train
    column_order = jnp.argsort(owner, stable=True)
    slot_code = (
        (jnp.take(train_ids, column_order) % local_train)
        .astype(jnp.float32)
        .reshape(1, local_train)
    )
    summed = lax.psum(scores, "layer")
    arrived, arrived_slots = (
        lax.all_to_all(
            jnp.take(summed, column_order, axis=1), "blk", split_axis=1, concat_axis=1, tiled=True
        ),
        lax.all_to_all(slot_code, "blk", split_axis=1, concat_axis=1, tiled=True),
    )
    result = place_columns(arrived, arrived_slots)
    return result


def solution(mesh):
    in_specs = (
        P("layer", None, "blk"),
        P(),
        P("layer", None, "blk"),
        P("layer", "blk"),
        P("layer", "blk", None),
        P("blk"),
    )
    out_specs = P(None, "blk")
    return jax.shard_map(
        on_device, mesh=mesh, in_specs=in_specs, out_specs=out_specs, check_vma=False
    )
```

profile of v0, /device:TPU:1, one launch (start us, length us, event | category | flops | bytes accessed | tf_op | source)
XLA Modules:
  0.0 470.0 jit_solution(16486788774307255985)
XLA Ops:
  6.5 0.0 copy-start
  6.5 0.0 copy-start.1
  6.5 0.8 and_select_fusion
  7.4 3.2 sort.31
  10.6 2.0 gather_fusion.1
  12.6 0.1 select_n.59
  12.6 0.1 copy.14
  12.7 0.7 copy.17
  13.4 14.4 %all-to-all-start.1 = ((f32[1,32,8]{2,0,1:T(1,128)}), f32[1,32,8]{2,0,1:T(1,128)S(1)}, u32[]{:S(2)}, u32[]{:S(2)}) async-start(f32[1,32,8]{2,0,1:T(1,128)} %copy.17), calls=%async_computation.1 | async-start | bytes 32768 | tf_op jit(solution)/shard_map/all_to_all | solution.py:49
  27.8 0.0 all-reduce.3.cloned.1.call-start
  27.9 0.7 compare_select_fusion.2
  28.6 0.7 compare_and_fusion.2
  29.2 1.5 gather_fusion
  30.7 0.1 broadcast_select_fusion
  30.8 1.3 reduce_sum.9
  32.0 49.1 %all_gather.3 = bf16[64,4096]{1,0:T(8,128)(2,1)} all-gather(bf16[64,128]{1,0:T(8,128)(2,1)S(1)} %broadcast_select_fusion), channel_id=1, replica_groups=mesh['layer'=16,'blk'=32] {'blk'}, dimensions={1}, use_global_device_ids=true | all-gather | bytes 540672 | tf_op jit(solution)/shard_map/all_gather | solution.py:25
  81.1 70.0 %psum.21 = f32[]{:T(128)} all-reduce(f32[]{:T(128)} %reduce_sum.9), channel_id=1, replica_groups=mesh['layer'=16,'blk'=32] {'blk'}, use_global_device_ids=true, to_apply=%region_1.2 | all-reduce | flops 1 | bytes 8 | tf_op jit(solution)/shard_map/psum | solution.py:22
  151.8 0.7 add_bitcast_fusion
  152.5 0.0 copy-done.1
  152.5 2.8 fusion.3
  155.2 144.0 %all-reduce.4 = bf16[64,4096]{1,0:T(8,128)(2,1)S(1)} all-reduce(f32[64,4096]{1,0:T(8,128)} %fusion.3), channel_id=1, replica_groups=mesh['layer'=16,'blk'=32] {'blk'}, use_global_device_ids=true, to_apply=%region_2.3 | all-reduce | flops 262144 | bytes 1572864 | tf_op jit(solution)/shard_map/psum | solution.py:33
  299.3 0.0 copy-done
  299.3 1.4 fusion
  300.7 0.0 all-reduce.3.cloned.1.call-update
  300.7 0.0 all-to-all-done.1
  300.7 0.1 convert_reduce_fusion
  300.8 0.1 convert_element_type.27
  300.9 3.1 sort.32
  304.0 123.2 %all-reduce.3.cloned.1.call-done = f32[64,256]{1,0:T(8,128)} async-done(((f32[64,256]{1,0:T(8,128)}), f32[64,256]{1,0:T(8,128)}) %all-reduce.3.cloned.1.call-update) | async-done | bytes 65552 | tf_op jit(solution)/shard_map/psum | solution.py:44
  427.2 0.9 copy.18
  428.1 0.7 gather_fusion.2
  428.9 0.1 fusion.10
  429.0 0.8 reshape.126
  429.7 20.5 %all-to-all-start = ((f32[32,1,512]{2,1,0:T(1,128)}), f32[32,1,512]{2,1,0:T(1,128)S(1)}, u32[]{:S(2)}, u32[]{:S(2)}) async-start(f32[32,1,512]{2,1,0:T(1,128)} %reshape.126), calls=%async_computation | async-start | bytes 131072 | tf_op jit(solution)/shard_map/all_to_all | solution.py:46
  450.3 9.9 %all-to-all-done = f32[32,1,512]{2,1,0:T(1,128)S(1)} async-done(((f32[32,1,512]{2,1,0:T(1,128)}), f32[32,1,512]{2,1,0:T(1,128)S(1)}, u32[]{:S(2)}, u32[]{:S(2)}) %all-to-all-start) | async-done | bytes 65568 | tf_op jit(solution)/shard_map/all_to_all | solution.py:46
  460.2 0.5 broadcast.118
  460.7 0.8 reduce.5
  461.5 0.1 reshape.127
  461.6 0.7 gather_fusion.3
  462.4 0.1 select_bitcast_fusion
  462.5 0.7 copy.19
  (11 shorter events, 0.1 us)
Async XLA Ops:
  6.5 292.7 %copy-start = (bf16[1,256,4096]{2,1,0:T(8,128)(2,1)S(1)}, bf16[1,256,4096]{2,1,0:T(8,128)(2,1)}, u32[]{:S(2)}) copy-start(bf16[1,256,4096]{2,1,0:T(8,128)(2,1)} %param.12) | copy-start | bytes 6291460
  6.5 145.9 %copy-start.1 = (bf16[1,4096,128]{2,1,0:T(8,128)(2,1)S(1)}, bf16[1,4096,128]{2,1,0:T(8,128)(2,1)}, u32[]{:S(2)}) copy-start(bf16[1,4096,128]{2,1,0:T(8,128)(2,1)} %param.10) | copy-start | bytes 3145732
  13.4 287.3 %all-to-all-start.1 = ((f32[1,32,8]{2,0,1:T(1,128)}), f32[1,32,8]{2,0,1:T(1,128)S(1)}, u32[]{:S(2)}, u32[]{:S(2)}) async-start(f32[1,32,8]{2,0,1:T(1,128)} %copy.17), calls=%async_computation.1 | async-start | bytes 32768 | tf_op jit(solution)/shard_map/all_to_all | solution.py:49
  27.8 399.4 %all-reduce.3.cloned.1.call-start = ((), (), s32[]{:S(2)}) async-start(), calls=%async_computation.2 | async-start | bytes 131072 | tf_op jit(solution)/shard_map/psum | solution.py:44
  429.7 30.5 %all-to-all-start = ((f32[32,1,512]{2,1,0:T(1,128)}), f32[32,1,512]{2,1,0:T(1,128)S(1)}, u32[]{:S(2)}, u32[]{:S(2)}) async-start(f32[32,1,512]{2,1,0:T(1,128)} %reshape.126), calls=%async_computation | async-start | bytes 131072 | tf_op jit(solution)/shard_map/all_to_all | solution.py:46
Sparse Core Ops, SparseCore 0:
  300.8 126.3 all-reduce.2
where the time goes:
time: 471 us; the launch traced here: 470 us
  blocking collectives  263 us (56%)
  waiting for transfers between devices  133 us (28%)
  starting transfers between devices  34.9 us (7%)
  between operations  14.2 us (3%)
  other arithmetic  11.6 us (2%)
  local copies, waits for them, and re-layouts  8.85 us (2%)
    psum x1, blocking collectives, on_device(): precond = lax.psum(partial_terms, 'blk').astype(jnp.bfloat16)  144 us
    psum x1, waiting for transfers between devices, on_device(): summed = lax.psum(scores, 'layer')  123 us
    psum x1, blocking collectives, on_device(): eigen_sum = lax.psum(jnp.sum(eigen_vals), 'blk')  70 us
    all_gather x1, blocking collectives, on_device(): lax.all_gather(selected, 'blk', axis=1, tiled=True)  49.1 us
    all_to_all x1, starting transfers between devices, on_device(): lax.all_to_all(jnp.take(summed, column_order, axis=1), 'blk', split_axis=...  20.5 us
    all_to_all x1, starting transfers between devices, on_device(): lax.all_to_all(slot_code, 'blk', split_axis=1, concat_axis=1, tiled=True)  14.4 us
    all_to_all x1, waiting for transfers between devices, on_device(): lax.all_to_all(jnp.take(summed, column_order, axis=1), 'blk', split_axis=...  9.95 us
  transfers between devices with their start and end apart: 3, of which 2 were waited for; matrix products, arithmetic and copies ran while one was open for 3% of the time, Pallas kernels for 0%

commit v1 on v0

v1 whole, which is shorter than its diff:
```python
import jax
import jax.numpy as jnp
from jax import lax
from jax.experimental import pallas as pl
from jax.experimental.pallas import tpu as pltpu
from jax.sharding import PartitionSpec as P

WIDTH = 4096
QUERIES = 64
LAYERS = 16
CHIPS = 16
CORES = 2
BLOCK = 128
HALF = CHIPS * BLOCK
ROWS = 256
MESH = pl.DeviceIdType.MESH
F32 = jnp.float32
BF16 = jnp.bfloat16


def split3(value):
    first = value.astype(BF16)
    rest = value - first.astype(F32)
    second = rest.astype(BF16)
    third = (rest - second.astype(F32)).astype(BF16)
    return first, second, third


def dot(a, b, a_dim, b_dim):
    return lax.dot_general(a, b, (((a_dim,), (b_dim,)), ((), ())), preferred_element_type=F32)


def owner_order(ids):
    owner = ids // ROWS
    slot = ids - owner * ROWS
    member = (lax.broadcasted_iota(jnp.int32, (32, ROWS), 0) == owner).astype(F32)
    before = lax.broadcasted_iota(jnp.int32, (ROWS, ROWS), 0) < lax.broadcasted_iota(jnp.int32, (ROWS, ROWS), 1)
    counts = dot(member.astype(BF16), before.astype(F32).astype(BF16), 1, 0)
    rank = jnp.sum(member * counts, axis=0, keepdims=True)
    place = owner * 8 + rank.astype(jnp.int32)
    hit = lax.broadcasted_iota(jnp.int32, (ROWS, ROWS), 0) == place
    slots = jnp.sum(jnp.where(hit, slot.astype(F32), 0.0), axis=1, keepdims=True)
    return hit.astype(F32).astype(BF16), slots


def kernel(
    pool_hbm, qids_hbm, eigen_hbm, evals_hbm, train_hbm, tids_hbm, out_ref,
    pool, qids, evals, ids, basis, train, sorted_train, gathered, message, pair_send, pair_recv,
    slots, back_send, back_recv, piece, precond, scores, layer_recv, tile, final,
    local_sem, basis_sem, train_sem, ids_sem, gather_sem, pair_sem, back_sem, precond_sem, layer_sem, final_sem,
):
    layer = lax.axis_index("layer")
    blk = lax.axis_index("blk")
    chip = blk // CORES
    core = blk - chip * CORES
    twin = chip * CORES + (1 - core)

    def peer(step):
        z_hi = chip // 4
        x = chip - z_hi * 4
        dz = (step // 4 + 2) % 4
        dx = (step + 2) % 4
        return ((z_hi + dz) % 4) * 4 + (x + dx) % 4

    others = [step for step in range(16) if step != 10]

    def remote(src, dst, send, recv, to_layer, to_blk):
        return pltpu.make_async_remote_copy(
            src_ref=src, dst_ref=dst, send_sem=send, recv_sem=recv,
            device_id=(to_layer, to_blk), device_id_type=MESH,
        )

    def drain(ref, sem):
        pltpu.make_async_copy(ref, ref, sem).wait()

    small = [
        pltpu.make_async_copy(pool_hbm.at[0], pool, local_sem.at[0]),
        pltpu.make_async_copy(qids_hbm, qids, local_sem.at[1]),
        pltpu.make_async_copy(evals_hbm, evals, local_sem.at[2]),
        pltpu.make_async_copy(tids_hbm, ids.at[core], local_sem.at[3]),
    ]
    for copy in small:
        copy.start()
    own_columns = pl.ds(pl.multiple_of(core * BLOCK, BLOCK), BLOCK)
    own_basis = pltpu.make_async_copy(eigen_hbm.at[0, :, core], basis.at[:, :, own_columns], local_sem.at[4])
    own_basis.start()

    barrier = pltpu.get_barrier_semaphore()
    for step in others:
        pl.semaphore_signal(barrier, inc=1, device_id=(layer, peer(step) * CORES + core), device_id_type=MESH)
    for step in range(LAYERS):
        other = lax.rem(layer + step, LAYERS)
        if step > 0:
            pl.semaphore_signal(barrier, inc=1, device_id=(other, blk), device_id_type=MESH)
        pl.semaphore_signal(barrier, inc=1, device_id=(other, twin), device_id_type=MESH)
    for step in range(CHIPS):
        source = lax.rem(chip + step, CHIPS) * CORES + core
        if step == 0:
            @pl.when(layer != chip)
            def _():
                pl.semaphore_signal(barrier, inc=1, device_id=(chip, source), device_id_type=MESH)
        else:
            pl.semaphore_signal(barrier, inc=1, device_id=(chip, source), device_id_type=MESH)

    for copy in small:
        copy.wait()
    pick = (lax.broadcasted_iota(jnp.int32, (256, QUERIES), 0) == qids[...]).astype(F32).astype(BF16)
    selected = dot(pick, pool[...], 0, 0).astype(BF16)
    first, second, third = split3(evals[...])
    message[0:QUERIES, :] = selected
    row = lax.broadcasted_iota(jnp.int32, (16, BLOCK), 0)
    terms = jnp.where(row == 0, first.astype(F32), jnp.where(row == 1, second.astype(F32), jnp.where(row == 2, third.astype(F32), 0.0)))
    message[QUERIES : QUERIES + 16, :] = terms.astype(BF16)
    own_features = pl.ds(pl.multiple_of(chip * BLOCK, BLOCK), BLOCK)
    gathered[:, own_features] = message[...]

    pl.semaphore_wait(barrier, 15 + 31 + 15 + (layer != chip).astype(jnp.int32))

    send_basis = remote(
        eigen_hbm.at[0, :, 1 - core], basis.at[:, :, own_columns], basis_sem.at[0], basis_sem.at[1], layer, twin
    )
    send_basis.start()
    for step in others:
        remote(
            message, gathered.at[:, own_features], gather_sem.at[0], gather_sem.at[1], layer, peer(step) * CORES + core
        ).start()
    send_ids = remote(ids.at[core], ids.at[core], ids_sem.at[0], ids_sem.at[1], layer, twin)
    send_ids.start()
    own_rows = pl.ds(pl.multiple_of(core * ROWS, ROWS), ROWS)
    for index in range(CHIPS):
        to_columns = pl.ds(index * BLOCK, BLOCK)
        kept = pl.ds(pl.multiple_of((index * CORES + core) * BLOCK, BLOCK), BLOCK)
        sent = pl.ds(pl.multiple_of((index * CORES + 1 - core) * BLOCK, BLOCK), BLOCK)
        pltpu.make_async_copy(train_hbm.at[0, :, kept], train.at[own_rows, to_columns], train_sem.at[0]).start()
        remote(
            train_hbm.at[0, :, sent], train.at[own_rows, to_columns], train_sem.at[1], train_sem.at[2], layer, twin
        ).start()

    send_ids.wait()
    hit_0, slots_0 = owner_order(ids[0])
    hit_1, slots_1 = owner_order(ids[1])
    lane = lax.broadcasted_iota(jnp.int32, (ROWS, BLOCK), 1)
    slots[...] = jnp.where(lane < QUERIES, slots_0, slots_1)

    own_basis.wait()
    send_basis.wait()
    drain(gathered.at[:, pl.ds(0, 15 * BLOCK)], gather_sem.at[1])
    rotated = dot(gathered[0:QUERIES, :], basis[...].reshape(HALF, CORES * BLOCK), 1, 0)
    total = jnp.sum(gathered[QUERIES : QUERIES + 16, :].astype(F32), keepdims=True)
    pair_send[0:QUERIES, :] = rotated
    pair_lane = lax.broadcasted_iota(jnp.int32, (8, CORES * BLOCK), 1)
    pair_row = lax.broadcasted_iota(jnp.int32, (8, CORES * BLOCK), 0)
    mine = pair_lane // BLOCK == core
    wide = jnp.concatenate([evals[...], evals[...]], axis=1)
    pair_send[QUERIES : QUERIES + 8, :] = jnp.where(
        pair_row == 0, jnp.where(mine, wide, 0.0), jnp.where(pair_row == 1, total, 0.0)
    )
    send_pair = remote(pair_send, pair_recv, pair_sem.at[0], pair_sem.at[1], layer, twin)
    send_pair.start()
    send_pair.wait()
    both = pair_send[...] + pair_recv[...]
    damping = 0.1 * both[QUERIES + 1 : QUERIES + 2, :] / WIDTH
    damped = (both[0:QUERIES, :] / (both[QUERIES : QUERIES + 1, :] + damping)).astype(BF16)

    def back_piece(target):
        return dot(damped, basis[target], 1, 1)

    def slot_rows(target):
        rows = slots[pl.ds(pl.multiple_of((target * CORES + core) * 8, 8), 8), :]
        return jnp.concatenate([rows, jnp.zeros_like(rows)], axis=0).astype(BF16)

    for step in others:
        target = peer(step)
        back_send[target, 0:QUERIES, :] = back_piece(target).astype(BF16)
        back_send[target, QUERIES : QUERIES + 16, :] = slot_rows(target)
        remote(
            back_send.at[target], back_recv.at[chip], back_sem.at[0], back_sem.at[1], layer, target * CORES + core
        ).start()
    own_piece = back_piece(chip)
    back_recv[chip, 0:QUERIES, :] = jnp.zeros((QUERIES, BLOCK), BF16)
    back_recv[chip, QUERIES : QUERIES + 16, :] = slot_rows(chip)

    drain(train.at[pl.ds(0, ROWS), :], train_sem.at[0])
    drain(train.at[pl.ds(0, ROWS), :], train_sem.at[1])
    drain(train.at[pl.ds(0, ROWS), :], train_sem.at[2])
    for index in range(CHIPS // 4):
        columns = pl.ds(index * 4 * BLOCK, 4 * BLOCK)
        sorted_train[0:ROWS, columns] = dot(hit_0, train[0:ROWS, columns], 1, 0).astype(BF16)
        sorted_train[ROWS : 2 * ROWS, columns] = dot(hit_1, train[ROWS : 2 * ROWS, columns], 1, 0).astype(BF16)

    drain(back_recv.at[pl.ds(0, 15)], back_sem.at[1])
    precond_piece = own_piece + jnp.sum(back_recv[:, 0:QUERIES, :].astype(F32), axis=0)
    piece[...] = precond_piece.astype(BF16)
    precond[:, own_features] = piece[...]
    for step in others:
        remote(
            piece, precond.at[:, own_features], precond_sem.at[0], precond_sem.at[1], layer, peer(step) * CORES + core
        ).start()

    arriving = back_recv[:, QUERIES : QUERIES + 16, :].astype(F32)[:, 0:8, :].reshape(BLOCK, BLOCK)
    id_lane = lax.broadcasted_iota(jnp.int32, (BLOCK, ROWS), 1).astype(F32)
    put_0 = (arriving[:, 0:1] == id_lane).astype(F32).astype(BF16)
    put_1 = (arriving[:, QUERIES : QUERIES + 1] == id_lane).astype(F32).astype(BF16)

    drain(precond.at[:, pl.ds(0, 15 * BLOCK)], precond_sem.at[1])
    queries = precond[...]
    nothing = jnp.zeros_like(queries)
    scores[...] = dot(sorted_train[0:ROWS, :], jnp.concatenate([queries, nothing], axis=0), 1, 1) + dot(
        sorted_train[ROWS : 2 * ROWS, :], jnp.concatenate([nothing, queries], axis=0), 1, 1
    )
    mine_at = layer * CORES + core
    for step in range(LAYERS):
        other = lax.rem(layer + step, LAYERS)
        for flip in range(CORES):
            if step == 0 and flip == 0:
                continue
            to_core = core if flip == 0 else 1 - core
            rows = pl.ds(pl.multiple_of((other * CORES + to_core) * 8, 8), 8)
            remote(
                scores.at[rows, :], layer_recv.at[mine_at], layer_sem.at[0], layer_sem.at[1],
                other, chip * CORES + to_core,
            ).start()
    layer_recv[mine_at] = scores[pl.ds(pl.multiple_of(mine_at * 8, 8), 8), :]
    drain(layer_recv.at[pl.ds(0, 31)], layer_sem.at[1])
    tile[...] = jnp.sum(layer_recv[...], axis=0)

    owner = layer * CORES + core
    for step in range(1, LAYERS):
        other = lax.rem(layer + step, LAYERS)
        remote(tile, final.at[chip], final_sem.at[0], final_sem.at[1], other, owner).start()

    @pl.when(layer != chip)
    def _():
        remote(tile, final.at[chip], final_sem.at[2], final_sem.at[1], layer, owner).start()

    @pl.when(layer == chip)
    def _():
        pltpu.make_async_copy(tile, final.at[chip], final_sem.at[1]).start()

    drain(final, final_sem.at[1])
    values = final[...].reshape(BLOCK, BLOCK)
    placed_0 = jnp.zeros((BLOCK, ROWS), F32)
    placed_1 = jnp.zeros((BLOCK, ROWS), F32)
    for term in split3(values):
        placed_0 += dot(term, put_0, 0, 0)
        placed_1 += dot(term, put_1, 0, 0)
    out_ref[...] = placed_0[0:QUERIES, :] + placed_1[QUERIES : 2 * QUERIES, :]

    drain(gathered.at[:, pl.ds(0, 15 * BLOCK)], gather_sem.at[0])
    drain(back_send.at[pl.ds(0, 15)], back_sem.at[0])
    drain(precond.at[:, pl.ds(0, 15 * BLOCK)], precond_sem.at[0])
    drain(layer_recv.at[pl.ds(0, 31)], layer_sem.at[0])
    drain(final.at[pl.ds(0, 15)], final_sem.at[0])

    @pl.when(layer != chip)
    def _():
        drain(tile, final_sem.at[2])


def on_device(query_pool, query_ids, eigenbasis, eigenvalues, train_grads, train_ids):
    return pl.pallas_call(
        kernel,
        out_shape=jax.ShapeDtypeStruct((QUERIES, ROWS), F32),
        in_specs=[pl.BlockSpec(memory_space=pl.ANY)] * 6,
        out_specs=pl.BlockSpec(memory_space=pltpu.VMEM),
        scratch_shapes=[
            pltpu.VMEM((256, BLOCK), BF16),
            pltpu.VMEM((1, QUERIES), jnp.int32),
            pltpu.VMEM((1, BLOCK), F32),
            pltpu.VMEM((CORES, 1, ROWS), jnp.int32),
            pltpu.VMEM((CHIPS, BLOCK, CORES * BLOCK), BF16),
            pltpu.VMEM((CORES * ROWS, HALF), BF16),
            pltpu.VMEM((CORES * ROWS, HALF), BF16),
            pltpu.VMEM((QUERIES + 16, HALF), BF16),
            pltpu.VMEM((QUERIES + 16, BLOCK), BF16),
            pltpu.VMEM((QUERIES + 8, CORES * BLOCK), F32),
            pltpu.VMEM((QUERIES + 8, CORES * BLOCK), F32),
            pltpu.VMEM((ROWS, BLOCK), F32),
            pltpu.VMEM((CHIPS, QUERIES + 16, BLOCK), BF16),
            pltpu.VMEM((CHIPS, QUERIES + 16, BLOCK), BF16),
            pltpu.VMEM((QUERIES, BLOCK), BF16),
            pltpu.VMEM((QUERIES, HALF), BF16),
            pltpu.VMEM((ROWS, BLOCK), F32),
            pltpu.VMEM((CORES * LAYERS, 8, BLOCK), F32),
            pltpu.VMEM((8, BLOCK), F32),
            pltpu.VMEM((CHIPS, 8, BLOCK), F32),
            pltpu.SemaphoreType.DMA((5,)),
            pltpu.SemaphoreType.DMA((2,)),
            pltpu.SemaphoreType.DMA((3,)),
            pltpu.SemaphoreType.DMA((2,)),
            pltpu.SemaphoreType.DMA((2,)),
            pltpu.SemaphoreType.DMA((2,)),
            pltpu.SemaphoreType.DMA((2,)),
            pltpu.SemaphoreType.DMA((2,)),
            pltpu.SemaphoreType.DMA((2,)),
            pltpu.SemaphoreType.DMA((3,)),
        ],
        compiler_params=pltpu.CompilerParams(
            collective_id=0, has_side_effects=True, vmem_limit_bytes=48 * 1024 * 1024
        ),
        cost_estimate=pl.CostEstimate(flops=600_000_000, bytes_accessed=4_000_000, transcendentals=0),
    )(
        query_pool,
        query_ids.reshape(1, QUERIES),
        eigenbasis.reshape(1, CHIPS, CORES, BLOCK, BLOCK),
        eigenvalues,
        train_grads,
        train_ids.reshape(1, ROWS),
    )


def solution(mesh):
    in_specs = (
        P("layer", None, "blk"),
        P(),
        P("layer", None, "blk"),
        P("layer", "blk"),
        P("layer", "blk", None),
        P("blk"),
    )
    out_specs = P(None, "blk")
    return jax.shard_map(
        on_device, mesh=mesh, in_specs=in_specs, out_specs=out_specs, check_vma=False
    )
```

time: 471 us -> 66.7 us (0.14)
  blocking collectives: 263 us -> 0 us
  waiting for transfers between devices: 133 us -> 0 us
  Pallas kernels: 0 us -> 60.2 us
  starting transfers between devices: 34.9 us -> 0 us
  between operations: 14.2 us -> 0.02 us
  other arithmetic: 11.6 us -> 0 us
    psum x2 -> x0, blocking collectives: 214 us -> none  [the longest x1 144 us: on_device(): precond = lax.psum(partial_terms, 'blk').astype(jnp.bfloat16)]
    psum x1 -> x0, waiting for transfers between devices: 123 us -> none  [on_device(): summed = lax.psum(scores, 'layer')]
    pallas_call x0 -> x1, Pallas kernels: none -> 60.2 us  [on_device(): pl.pallas_call(kernel, out_shape=jax.ShapeDtypeStruct((QUERIES, ROWS), F3...]
    all_gather x1 -> x0, blocking collectives: 49.1 us -> none  [on_device(): lax.all_gather(selected, 'blk', axis=1, tiled=True)]
    all_to_all x2 -> x0, starting transfers between devices: 34.9 us -> none  [the longest x1 20.5 us: on_device(): lax.all_to_all(jnp.take(summed, column_order, axis=1), 'blk', split_axis=...]
    all_to_all x2 -> x0, waiting for transfers between devices: 9.95 us -> none  [the longest x1 9.95 us: on_device(): lax.all_to_all(jnp.take(summed, column_order, axis=1), 'blk', split_axis=...]
    sort x2 -> x0, other arithmetic: 6.31 us -> none  [the longest x1 3.17 us: on_device(): column_order = jnp.argsort(owner, stable=True)]
    unnamed x6 -> x13, local copies, waits for them, and re-layouts: 0.85 us -> 6.27 us
  transfers between devices with their start and end apart: 3 -> 0, of which waited for: 2 -> 0; matrix products, arithmetic and copies ran while one was open for 3% -> 0% of each run, Pallas kernels for 0% -> 0%
where the time goes in v1:
time: 66.7 us; the launch traced here: 66.5 us
  Pallas kernels  60.2 us (90%)
  local copies, waits for them, and re-layouts  6.27 us (9%)
    pallas_call x1, Pallas kernels, on_device(): pl.pallas_call(kernel, out_shape=jax.ShapeDtypeStruct((QUERIES, ROWS), F3...  60.2 us
    unnamed x13, local copies, waits for them, and re-layouts  6.27 us

profile of v1, /device:TPU:1, one launch (start us, length us, event | category | flops | bytes accessed | tf_op | source)
XLA Modules:
  0.0 66.5 jit_solution(12766798369135546626)
XLA Ops:
  0.0 0.0 copy-start
  0.0 1.6 %copy-done = bf16[1,256,4096]{2,1,0:T(8,128)(2,1)S(1)} copy-done((bf16[1,256,4096]{2,1,0:T(8,128)(2,1)S(1)}, bf16[1,256,4096]{2,1,0:T(8,128)(2,1)}, u32[]{:S(2)}) %copy-start) | copy-done | bytes 2097176
  1.6 0.0 copy-start.1
  1.6 1.2 %copy-done.1 = bf16[1,4096,128]{2,1,0:T(8,128)(2,1)S(1)} copy-done((bf16[1,4096,128]{2,1,0:T(8,128)(2,1)S(1)}, bf16[1,4096,128]{2,1,0:T(8,128)(2,1)}, u32[]{:S(2)}) %copy-start.1) | copy-done | bytes 1048600
  2.8 0.0 copy-start.2
  2.8 0.8 %copy-done.2 = bf16[1,256,128]{2,1,0:T(8,128)(2,1)S(1)} copy-done((bf16[1,256,128]{2,1,0:T(8,128)(2,1)S(1)}, bf16[1,256,128]{2,1,0:T(8,128)(2,1)}, u32[]{:S(2)}) %copy-start.2) | copy-done | bytes 65560
  3.7 0.0 copy-start.3
  3.7 0.7 %copy-done.3 = s32[256]{0:T(256)S(1)} copy-done((s32[256]{0:T(256)S(1)}, s32[256]{0:T(256)}, u32[]{:S(2)}) %copy-start.3) | copy-done | bytes 1048
  4.3 0.0 copy-start.4
  4.3 0.7 copy-done.4
  5.0 0.0 copy-start.5
  5.0 0.7 copy-done.5
  5.6 60.2 %shard_map.64 = f32[64,256]{1,0:T(8,128)S(1)} custom-call(bf16[1,256,128]{2,1,0:T(8,128)(2,1)S(1)} %copy-done.2, s32[1,64]{1,0:T(1,128)S(1)} %bitcast.5, bf16[1,16,2,128,128]{4,3,2,1,0:T(8,128)(2,1)S(1)} %bitcast.3, f32[1,128]{1,0:T(1,128)S(1)} %copy-done.5, bf16[1,256,4096]{2,1,0:T(8,128)(2,1)S(1)} %copy-done, s32[1,256]{1,0:T(1,128)S(1)} %bitcast.4), custom_call_target="tpu_custom_call" | custom-call | flops 600000000 | bytes 4000000 | tf_op jit(solution)/shard_map/pallas_call | solution.py:261
  65.8 0.6 copy.8
Async XLA Ops:
  0.0 1.6 %copy-start = (bf16[1,256,4096]{2,1,0:T(8,128)(2,1)S(1)}, bf16[1,256,4096]{2,1,0:T(8,128)(2,1)}, u32[]{:S(2)}) copy-start(bf16[1,256,4096]{2,1,0:T(8,128)(2,1)} %train_hbm.1) | copy-start | bytes 6291460
  1.6 1.2 %copy-start.1 = (bf16[1,4096,128]{2,1,0:T(8,128)(2,1)S(1)}, bf16[1,4096,128]{2,1,0:T(8,128)(2,1)}, u32[]{:S(2)}) copy-start(bf16[1,4096,128]{2,1,0:T(8,128)(2,1)} %param.8) | copy-start | bytes 3145732
  2.8 0.8 %copy-start.2 = (bf16[1,256,128]{2,1,0:T(8,128)(2,1)S(1)}, bf16[1,256,128]{2,1,0:T(8,128)(2,1)}, u32[]{:S(2)}) copy-start(bf16[1,256,128]{2,1,0:T(8,128)(2,1)} %pool_hbm.1) | copy-start | bytes 196612
  3.7 0.7 %copy-start.3 = (s32[256]{0:T(256)S(1)}, s32[256]{0:T(256)}, u32[]{:S(2)}) copy-start(s32[256]{0:T(256)} %param.11) | copy-start | bytes 3076
  4.3 0.7 copy-start.4
  5.0 0.7 copy-start.5

commit v2 on v1

v2 whole, which is shorter than its diff:
```python
import jax
import jax.numpy as jnp
from jax import lax
from jax.experimental import pallas as pl
from jax.experimental.pallas import tpu as pltpu
from jax.sharding import PartitionSpec as P

WIDTH = 4096
QUERIES = 64
LAYERS = 16
CHIPS = 16
CORES = 2
SIDE = 4
LAYER_STEPS = (8, 9, 7, 10, 6, 11, 5, 12, 4, 13, 3, 14, 2, 15, 1, 0)
BLOCK = 128
ROWS = 256
MESH = pl.DeviceIdType.MESH
F32 = jnp.float32
BF16 = jnp.bfloat16


def split3(value):
    first = value.astype(BF16)
    rest = value - first.astype(F32)
    second = rest.astype(BF16)
    third = (rest - second.astype(F32)).astype(BF16)
    return first, second, third


def dot(a, b, a_dim, b_dim):
    return lax.dot_general(a, b, (((a_dim,), (b_dim,)), ((), ())), preferred_element_type=F32)


def owner_order(ids):
    owner = ids // ROWS
    slot = ids - owner * ROWS
    member = (lax.broadcasted_iota(jnp.int32, (32, ROWS), 0) == owner).astype(F32)
    before = lax.broadcasted_iota(jnp.int32, (ROWS, ROWS), 0) < lax.broadcasted_iota(jnp.int32, (ROWS, ROWS), 1)
    counts = dot(member.astype(BF16), before.astype(F32).astype(BF16), 1, 0)
    rank = jnp.sum(member * counts, axis=0, keepdims=True)
    place = owner * 8 + rank.astype(jnp.int32)
    hit = lax.broadcasted_iota(jnp.int32, (ROWS, ROWS), 0) == place
    return hit.astype(F32).astype(BF16), place * ROWS + slot


def kernel(
    pool_hbm, qids_hbm, eigen_hbm, evals_hbm, train_hbm, tids_hbm, out_ref,
    pool, qids, evals, ids, basis, train, sorted_train, gathered, message, all_evals, pair_send, pair_recv,
    codes, all_codes, back_send, back_recv, piece, precond, scores, layer_recv, tile, final,
    local_sem, basis_sem, train_sem, ids_sem, gather_sem, evals_sem, pair_sem, codes_sem, back_sem, precond_sem,
    layer_sem, final_sem,
):
    layer = lax.axis_index("layer")
    blk = lax.axis_index("blk")
    chip = blk // CORES
    core = blk - chip * CORES
    z_hi = chip // SIDE
    x = chip - z_hi * SIDE
    twin = chip * CORES + (1 - core)

    others = [
        (2, 2), (1, 2), (3, 2), (2, 1), (2, 3), (1, 1), (3, 3), (2, 0), (1, 3), (3, 1), (1, 0), (3, 0), (0, 2), (0, 1), (0, 3)
    ]

    def peer(dz, dx):
        return lax.rem(z_hi + dz, SIDE) * SIDE + lax.rem(x + dx, SIDE)

    def remote(src, dst, send, recv, to_layer, to_blk):
        return pltpu.make_async_remote_copy(
            src_ref=src, dst_ref=dst, send_sem=send, recv_sem=recv,
            device_id=(to_layer, to_blk), device_id_type=MESH,
        )

    def drain(ref, sem):
        pltpu.make_async_copy(ref, ref, sem).wait()

    barrier = pltpu.get_barrier_semaphore()
    for dz, dx in others:
        pl.semaphore_signal(barrier, inc=1, device_id=(layer, peer(dz, dx) * CORES + core), device_id_type=MESH)
    for step in range(LAYERS):
        other = lax.rem(layer + step, LAYERS)
        if step > 0:
            pl.semaphore_signal(barrier, inc=1, device_id=(other, blk), device_id_type=MESH)
        pl.semaphore_signal(barrier, inc=1, device_id=(other, twin), device_id_type=MESH)

    small = [
        pltpu.make_async_copy(pool_hbm.at[0], pool, local_sem.at[0]),
        pltpu.make_async_copy(qids_hbm, qids, local_sem.at[1]),
        pltpu.make_async_copy(evals_hbm, evals, local_sem.at[2]),
        pltpu.make_async_copy(tids_hbm, ids.at[core], local_sem.at[3]),
    ]
    for copy in small:
        copy.start()
    own_columns = pl.ds(pl.multiple_of(core * BLOCK, BLOCK), BLOCK)
    own_basis = pltpu.make_async_copy(eigen_hbm.at[0, :, core], basis.at[:, :, own_columns], local_sem.at[4])
    own_basis.start()
    own_rows = pl.ds(pl.multiple_of(core * ROWS, ROWS), ROWS)
    for index in range(CHIPS):
        kept = pl.ds(pl.multiple_of((index * CORES + core) * BLOCK, BLOCK), BLOCK)
        to_columns = pl.ds((index % SIDE) * BLOCK, BLOCK)
        pltpu.make_async_copy(
            train_hbm.at[0, :, kept], train.at[index // SIDE, own_rows, to_columns], train_sem.at[0]
        ).start()

    for copy in small:
        copy.wait()
    pick = (lax.broadcasted_iota(jnp.int32, (256, QUERIES), 0) == qids[...]).astype(F32).astype(BF16)
    message[...] = dot(pick, pool[...], 0, 0).astype(BF16)
    own_features = pl.ds(pl.multiple_of(x * BLOCK, BLOCK), BLOCK)
    gathered[z_hi, :, own_features] = message[...]
    all_evals[chip] = evals[...]

    pl.semaphore_wait(barrier, 15 + 31)

    send_basis = remote(
        eigen_hbm.at[0, :, 1 - core], basis.at[:, :, own_columns], basis_sem.at[0], basis_sem.at[1], layer, twin
    )
    send_basis.start()
    for dz, dx in others:
        target = peer(dz, dx) * CORES + core
        remote(
            message, gathered.at[z_hi, :, own_features], gather_sem.at[0], gather_sem.at[1 + dz], layer, target
        ).start()
    for dz, dx in others:
        target = peer(dz, dx) * CORES + core
        remote(evals, all_evals.at[chip], evals_sem.at[0], evals_sem.at[1], layer, target).start()
    send_ids = remote(ids.at[core], ids.at[core], ids_sem.at[0], ids_sem.at[1], layer, twin)
    send_ids.start()
    for index in range(CHIPS):
        sent = pl.ds(pl.multiple_of((index * CORES + 1 - core) * BLOCK, BLOCK), BLOCK)
        to_columns = pl.ds((index % SIDE) * BLOCK, BLOCK)
        remote(
            train_hbm.at[0, :, sent], train.at[index // SIDE, own_rows, to_columns],
            train_sem.at[1], train_sem.at[2], layer, twin,
        ).start()

    send_ids.wait()
    hit_0, codes_0 = owner_order(ids[0])
    hit_1, codes_1 = owner_order(ids[1])
    codes[0] = codes_0
    codes[1] = codes_1
    all_codes[chip, 0] = codes_0
    all_codes[chip, 1] = codes_1

    own_basis.wait()
    send_basis.wait()

    def row_of(dz):
        return lax.rem(z_hi + (SIDE - dz), SIDE)

    rotated = jnp.zeros((QUERIES, CORES * BLOCK), F32)
    for dz in (0, 1, 3, 2):
        row = row_of(dz)
        if dz == 0:
            drain(gathered.at[0, :, pl.ds(0, 3 * BLOCK)], gather_sem.at[1])
        else:
            drain(gathered.at[0], gather_sem.at[1 + dz])
        rows = basis[pl.ds(row * SIDE, SIDE)].reshape(SIDE * BLOCK, CORES * BLOCK)
        rotated += dot(gathered[row], rows, 1, 0)
    drain(all_evals.at[pl.ds(0, 15)], evals_sem.at[1])
    total = jnp.sum(all_evals[...][:, 0, :], keepdims=True)
    pair_send[0:QUERIES, :] = rotated
    pair_lane = lax.broadcasted_iota(jnp.int32, (8, CORES * BLOCK), 1)
    pair_row = lax.broadcasted_iota(jnp.int32, (8, CORES * BLOCK), 0)
    mine = pair_lane // BLOCK == core
    wide = jnp.concatenate([evals[...], evals[...]], axis=1)
    pair_send[QUERIES : QUERIES + 8, :] = jnp.where(
        pair_row == 0, jnp.where(mine, wide, 0.0), jnp.where(pair_row == 1, total, 0.0)
    )
    send_pair = remote(pair_send, pair_recv, pair_sem.at[0], pair_sem.at[1], layer, twin)
    send_pair.start()
    for dz, dx in others:
        target = peer(dz, dx) * CORES + core
        remote(codes, all_codes.at[chip], codes_sem.at[0], codes_sem.at[1], layer, target).start()
    send_pair.wait()
    both = pair_send[...] + pair_recv[...]
    damping = 0.1 * both[QUERIES + 1 : QUERIES + 2, :] / WIDTH
    damped = (both[0:QUERIES, :] / (both[QUERIES : QUERIES + 1, :] + damping)).astype(BF16)

    for dz, dx in others:
        target = peer(dz, dx)
        back_send[target] = dot(damped, basis[target], 1, 1).astype(BF16)
        remote(
            back_send.at[target], back_recv.at[chip], back_sem.at[0], back_sem.at[1 + dz], layer, target * CORES + core
        ).start()
    precond_sum = dot(damped, basis[chip], 1, 1)
    back_recv[chip] = jnp.zeros((QUERIES, BLOCK), BF16)

    for sem in range(3):
        drain(train.at[:, pl.ds(0, ROWS), :], train_sem.at[sem])
    for index in range(SIDE):
        sorted_train[index, 0:ROWS, :] = dot(hit_0, train[index, 0:ROWS, :], 1, 0).astype(BF16)
        sorted_train[index, ROWS : 2 * ROWS, :] = dot(hit_1, train[index, ROWS : 2 * ROWS, :], 1, 0).astype(BF16)

    for dz in (0, 1, 3, 2):
        drain(back_recv.at[pl.ds(0, 3 if dz == 0 else 4)], back_sem.at[1 + dz])
        precond_sum += jnp.sum(back_recv[pl.ds(row_of(dz) * SIDE, SIDE)].astype(F32), axis=0)
    piece[...] = precond_sum.astype(BF16)
    precond[z_hi, :, own_features] = piece[...]
    for dz, dx in others:
        target = peer(dz, dx) * CORES + core
        remote(
            piece, precond.at[z_hi, :, own_features], precond_sem.at[0], precond_sem.at[1 + dz], layer, target
        ).start()

    total_scores = jnp.zeros((ROWS, BLOCK), F32)
    nothing = jnp.zeros((QUERIES, SIDE * BLOCK), BF16)
    for dz in (0, 1, 3, 2):
        row = row_of(dz)
        if dz == 0:
            drain(precond.at[0, :, pl.ds(0, 3 * BLOCK)], precond_sem.at[1])
        else:
            drain(precond.at[0], precond_sem.at[1 + dz])
        queries = precond[row]
        total_scores += dot(sorted_train[row, 0:ROWS, :], jnp.concatenate([queries, nothing], axis=0), 1, 1)
        total_scores += dot(sorted_train[row, ROWS : 2 * ROWS, :], jnp.concatenate([nothing, queries], axis=0), 1, 1)
    scores[...] = total_scores
    mine_at = layer * CORES + core
    for step in LAYER_STEPS:
        other = lax.rem(layer + step, LAYERS)
        for flip in range(CORES):
            if step == 0 and flip == 0:
                continue
            to_core = core if flip == 0 else 1 - core
            rows = pl.ds(pl.multiple_of((other * CORES + to_core) * 8, 8), 8)
            remote(
                scores.at[rows, :], layer_recv.at[mine_at], layer_sem.at[0], layer_sem.at[1],
                other, chip * CORES + to_core,
            ).start()
    layer_recv[mine_at] = scores[pl.ds(pl.multiple_of(mine_at * 8, 8), 8), :]

    drain(all_codes.at[pl.ds(0, 15)], codes_sem.at[1])
    rank = lax.broadcasted_iota(jnp.int32, (CHIPS, 8, ROWS), 1)
    lane = lax.broadcasted_iota(jnp.int32, (CHIPS, 8, ROWS), 2).astype(F32)
    put = []
    for source in range(CORES):
        code = all_codes[:, source]
        place = code // ROWS
        slot = (code - place * ROWS).astype(F32)
        wanted = jnp.sum(jnp.where(place - 8 * blk == rank, slot, 0.0), axis=2, keepdims=True)
        put.append((wanted == lane).astype(F32).reshape(BLOCK, ROWS).astype(BF16))

    drain(layer_recv.at[pl.ds(0, 31)], layer_sem.at[1])
    tile[...] = jnp.sum(layer_recv[...], axis=0)

    owner = layer * CORES + core
    for step in LAYER_STEPS:
        if step == 0:
            continue
        other = lax.rem(layer + step, LAYERS)
        remote(tile, final.at[chip], final_sem.at[0], final_sem.at[1], other, owner).start()

    @pl.when(layer != chip)
    def _():
        remote(tile, final.at[chip], final_sem.at[2], final_sem.at[1], layer, owner).start()

    @pl.when(layer == chip)
    def _():
        pltpu.make_async_copy(tile, final.at[chip], final_sem.at[1]).start()

    drain(final, final_sem.at[1])
    values = final[...].reshape(BLOCK, BLOCK)
    placed_0 = jnp.zeros((BLOCK, ROWS), F32)
    placed_1 = jnp.zeros((BLOCK, ROWS), F32)
    for term in split3(values):
        placed_0 += dot(term, put[0], 0, 0)
        placed_1 += dot(term, put[1], 0, 0)
    out_ref[...] = placed_0[0:QUERIES, :] + placed_1[QUERIES : 2 * QUERIES, :]

    for _ in range(5):
        drain(gathered.at[0, :, pl.ds(0, 3 * BLOCK)], gather_sem.at[0])
    drain(all_evals.at[pl.ds(0, 15)], evals_sem.at[0])
    drain(all_codes.at[pl.ds(0, 15)], codes_sem.at[0])
    drain(back_recv.at[pl.ds(0, 15)], back_sem.at[0])
    for _ in range(5):
        drain(precond.at[0, :, pl.ds(0, 3 * BLOCK)], precond_sem.at[0])
    drain(layer_recv.at[pl.ds(0, 31)], layer_sem.at[0])
    drain(final.at[pl.ds(0, 15)], final_sem.at[0])

    @pl.when(layer != chip)
    def _():
        drain(tile, final_sem.at[2])


def on_device(query_pool, query_ids, eigenbasis, eigenvalues, train_grads, train_ids):
    return pl.pallas_call(
        kernel,
        out_shape=jax.ShapeDtypeStruct((QUERIES, ROWS), F32),
        in_specs=[pl.BlockSpec(memory_space=pl.ANY)] * 6,
        out_specs=pl.BlockSpec(memory_space=pltpu.VMEM),
        scratch_shapes=[
            pltpu.VMEM((256, BLOCK), BF16),
            pltpu.VMEM((1, QUERIES), jnp.int32),
            pltpu.VMEM((1, BLOCK), F32),
            pltpu.VMEM((CORES, 1, ROWS), jnp.int32),
            pltpu.VMEM((CHIPS, BLOCK, CORES * BLOCK), BF16),
            pltpu.VMEM((SIDE, CORES * ROWS, SIDE * BLOCK), BF16),
            pltpu.VMEM((SIDE, CORES * ROWS, SIDE * BLOCK), BF16),
            pltpu.VMEM((SIDE, QUERIES, SIDE * BLOCK), BF16),
            pltpu.VMEM((QUERIES, BLOCK), BF16),
            pltpu.VMEM((CHIPS, 1, BLOCK), F32),
            pltpu.VMEM((QUERIES + 8, CORES * BLOCK), F32),
            pltpu.VMEM((QUERIES + 8, CORES * BLOCK), F32),
            pltpu.VMEM((CORES, 1, ROWS), jnp.int32),
            pltpu.VMEM((CHIPS, CORES, 1, ROWS), jnp.int32),
            pltpu.VMEM((CHIPS, QUERIES, BLOCK), BF16),
            pltpu.VMEM((CHIPS, QUERIES, BLOCK), BF16),
            pltpu.VMEM((QUERIES, BLOCK), BF16),
            pltpu.VMEM((SIDE, QUERIES, SIDE * BLOCK), BF16),
            pltpu.VMEM((ROWS, BLOCK), F32),
            pltpu.VMEM((CORES * LAYERS, 8, BLOCK), F32),
            pltpu.VMEM((8, BLOCK), F32),
            pltpu.VMEM((CHIPS, 8, BLOCK), F32),
            pltpu.SemaphoreType.DMA((5,)),
            pltpu.SemaphoreType.DMA((2,)),
            pltpu.SemaphoreType.DMA((3,)),
            pltpu.SemaphoreType.DMA((2,)),
            pltpu.SemaphoreType.DMA((5,)),
            pltpu.SemaphoreType.DMA((2,)),
            pltpu.SemaphoreType.DMA((2,)),
            pltpu.SemaphoreType.DMA((2,)),
            pltpu.SemaphoreType.DMA((5,)),
            pltpu.SemaphoreType.DMA((5,)),
            pltpu.SemaphoreType.DMA((2,)),
            pltpu.SemaphoreType.DMA((3,)),
        ],
        compiler_params=pltpu.CompilerParams(
            collective_id=0, has_side_effects=True, vmem_limit_bytes=40 * 1024 * 1024
        ),
        cost_estimate=pl.CostEstimate(flops=600_000_000, bytes_accessed=4_000_000, transcendentals=0),
    )(
        *[
            pltpu.with_memory_space_constraint(array, pltpu.HBM)
            for array in (
                query_pool,
                query_ids.reshape(1, QUERIES),
                eigenbasis.reshape(1, CHIPS, CORES, BLOCK, BLOCK),
                eigenvalues,
                train_grads,
                train_ids.reshape(1, ROWS),
            )
        ]
    )


def solution(mesh):
    in_specs = (
        P("layer", None, "blk"),
        P(),
        P("layer", None, "blk"),
        P("layer", "blk"),
        P("layer", "blk", None),
        P("blk"),
    )
    out_specs = P(None, "blk")
    return jax.shard_map(
        on_device, mesh=mesh, in_specs=in_specs, out_specs=out_specs, check_vma=False
    )
```

time: 66.7 us -> 58.6 us (0.88)
  local copies, waits for them, and re-layouts: 6.27 us -> 0.63 us
  Pallas kernels: 60.2 us -> 57.7 us
    unnamed x13 -> x1, local copies, waits for them, and re-layouts: 6.27 us -> 0.63 us
    pallas_call x1, Pallas kernels: 60.2 us -> 57.7 us  [on_device(): pl.pallas_call(kernel, out_shape=jax.ShapeDtypeStruct((QUERIES, ROWS), F3...]
where the time goes in v2:
time: 58.6 us; the launch traced here: 58.3 us
  Pallas kernels  57.7 us (98%)
  local copies, waits for them, and re-layouts  0.63 us (1%)
    pallas_call x1, Pallas kernels, on_device(): pl.pallas_call(kernel, out_shape=jax.ShapeDtypeStruct((QUERIES, ROWS), F3...  57.7 us

profile of v2, /device:TPU:1, one launch (start us, length us, event | category | flops | bytes accessed | tf_op | source)
XLA Modules:
  0.0 58.3 jit_solution(1325976524222344372)
XLA Ops:
  0.0 57.7 %shard_map.64 = f32[64,256]{1,0:T(8,128)S(1)} custom-call(bf16[1,256,128]{2,1,0:T(8,128)(2,1)} %pool_hbm.1, s32[1,64]{1,0:T(1,128)} %bitcast.5, bf16[1,16,2,128,128]{4,3,2,1,0:T(8,128)(2,1)} %bitcast.3, f32[1,128]{1,0:T(1,128)} %evals_hbm.1, bf16[1,256,4096]{2,1,0:T(8,128)(2,1)} %train_hbm.1, s32[1,256]{1,0:T(1,128)} %bitcast.4), custom_call_target="tpu_custom_call" | custom-call | flops 600000000 | bytes 4000000 | tf_op jit(solution)/shard_map/pallas_call | solution.py:286
  57.7 0.6 %copy.8 = f32[64,256]{1,0:T(8,128)} copy(f32[64,256]{1,0:T(8,128)S(1)} %shard_map.64) | data formatting | bytes 131072

commit v3 on v2

--- a/solution.py
+++ b/solution.py
@@ -7,6 +7,9 @@
 
 WIDTH = 4096
 QUERIES = 64
+PARTS = 2
+PART = QUERIES // PARTS
+LAG = 0
 LAYERS = 16
 CHIPS = 16
 CORES = 2
@@ -45,7 +48,7 @@
 
 def kernel(
     pool_hbm, qids_hbm, eigen_hbm, evals_hbm, train_hbm, tids_hbm, out_ref,
-    pool, qids, evals, ids, basis, train, sorted_train, gathered, message, all_evals, pair_send, pair_recv,
+    pool, qids, evals, ids, basis, train, sorted_train, gathered, message, all_evals, pair_evals, pair_send, pair_recv,
     codes, all_codes, back_send, back_recv, piece, precond, scores, layer_recv, tile, final,
     local_sem, basis_sem, train_sem, ids_sem, gather_sem, evals_sem, pair_sem, codes_sem, back_sem, precond_sem,
     layer_sem, final_sem,
@@ -105,25 +108,27 @@
     for copy in small:
         copy.wait()
     pick = (lax.broadcasted_iota(jnp.int32, (256, QUERIES), 0) == qids[...]).astype(F32).astype(BF16)
-    message[...] = dot(pick, pool[...], 0, 0).astype(BF16)
+    message[...] = dot(pick, pool[...], 0, 0).astype(BF16).reshape(PARTS, PART, BLOCK)
     own_features = pl.ds(pl.multiple_of(x * BLOCK, BLOCK), BLOCK)
-    gathered[z_hi, :, own_features] = message[...]
+    gathered[:, z_hi, :, own_features] = message[...]
     all_evals[chip] = evals[...]
 
     pl.semaphore_wait(barrier, 15 + 31)
 
-    send_basis = remote(
-        eigen_hbm.at[0, :, 1 - core], basis.at[:, :, own_columns], basis_sem.at[0], basis_sem.at[1], layer, twin
-    )
-    send_basis.start()
-    for dz, dx in others:
-        target = peer(dz, dx) * CORES + core
-        remote(
-            message, gathered.at[z_hi, :, own_features], gather_sem.at[0], gather_sem.at[1 + dz], layer, target
-        ).start()
     for dz, dx in others:
         target = peer(dz, dx) * CORES + core
         remote(evals, all_evals.at[chip], evals_sem.at[0], evals_sem.at[1], layer, target).start()
+    send_basis = remote(
+        eigen_hbm.at[0, :, 1 - core], basis.at[:, :, own_columns], basis_sem.at[0], basis_sem.at[1], layer, twin
+    )
+    send_basis.start()
+    for part in range(PARTS):
+        for dz, dx in others:
+            target = peer(dz, dx) * CORES + core
+            remote(
+                message.at[part], gathered.at[part, z_hi, :, own_features],
+                gather_sem.at[0], gather_sem.at[1 + part * SIDE + dz], layer, target,
+            ).start()
     send_ids = remote(ids.at[core], ids.at[core], ids_sem.at[0], ids_sem.at[1], layer, twin)
     send_ids.start()
     for index in range(CHIPS):
@@ -148,43 +153,69 @@
     def row_of(dz):
         return lax.rem(z_hi + (SIDE - dz), SIDE)
 
-    rotated = jnp.zeros((QUERIES, CORES * BLOCK), F32)
-    for dz in (0, 1, 3, 2):
-        row = row_of(dz)
-        if dz == 0:
-            drain(gathered.at[0, :, pl.ds(0, 3 * BLOCK)], gather_sem.at[1])
-        else:
-            drain(gathered.at[0], gather_sem.at[1 + dz])
-        rows = basis[pl.ds(row * SIDE, SIDE)].reshape(SIDE * BLOCK, CORES * BLOCK)
-        rotated += dot(gathered[row], rows, 1, 0)
     drain(all_evals.at[pl.ds(0, 15)], evals_sem.at[1])
     total = jnp.sum(all_evals[...][:, 0, :], keepdims=True)
-    pair_send[0:QUERIES, :] = rotated
     pair_lane = lax.broadcasted_iota(jnp.int32, (8, CORES * BLOCK), 1)
     pair_row = lax.broadcasted_iota(jnp.int32, (8, CORES * BLOCK), 0)
     mine = pair_lane // BLOCK == core
     wide = jnp.concatenate([evals[...], evals[...]], axis=1)
-    pair_send[QUERIES : QUERIES + 8, :] = jnp.where(
+    pair_evals[0] = jnp.where(
         pair_row == 0, jnp.where(mine, wide, 0.0), jnp.where(pair_row == 1, total, 0.0)
     )
-    send_pair = remote(pair_send, pair_recv, pair_sem.at[0], pair_sem.at[1], layer, twin)
-    send_pair.start()
+    send_evals = remote(pair_evals.at[0], pair_evals.at[1], evals_sem.at[2], evals_sem.at[3], layer, twin)
+    send_evals.start()
+
+    send_pair = []
+    own_parts = []
+
+    def rotate(part):
+        rotated = jnp.zeros((PART, CORES * BLOCK), F32)
+        for dz in (0, 1, 3, 2):
+            row = row_of(dz)
+            arrival = gather_sem.at[1 + part * SIDE + dz]
+            if dz == 0:
+                drain(gathered.at[part, 0, :, pl.ds(0, 3 * BLOCK)], arrival)
+            else:
+                drain(gathered.at[part, 0], arrival)
+            rows = basis[pl.ds(row * SIDE, SIDE)].reshape(SIDE * BLOCK, CORES * BLOCK)
+            rotated += dot(gathered[part, row], rows, 1, 0)
+        pair_send[part] = rotated
+        send_pair.append(
+            remote(pair_send.at[part], pair_recv.at[part], pair_sem.at[0], pair_sem.at[1 + part], layer, twin)
+        )
+        send_pair[part].start()
+
+    def send_back(part):
+        send_pair[part].wait_recv()
+        damped = ((pair_send[part] + pair_recv[part]) / divisor).astype(BF16)
+        for dz in (2, 1, 3, 0):
+            row = lax.rem(z_hi + dz, SIDE)
+            rows = basis[pl.ds(row * SIDE, SIDE)].reshape(SIDE * BLOCK, CORES * BLOCK)
+            back_send[part, row] = dot(damped, rows, 1, 1).astype(BF16)
+            for dx in (2, 1, 3, 0):
+                if dz == 0 and dx == 0:
+                    continue
+                column = lax.rem(x + dx, SIDE)
+                block = pl.ds(pl.multiple_of(column * BLOCK, BLOCK), BLOCK)
+                remote(
+                    back_send.at[part, row, :, block], back_recv.at[part, chip],
+                    back_sem.at[0], back_sem.at[1 + part * SIDE + dz], layer, (row * SIDE + column) * CORES + core,
+                ).start()
+        own_parts.append(dot(damped, basis[chip], 1, 1))
+        back_recv[part, chip] = jnp.zeros((PART, BLOCK), BF16)
+
+    for part in range(PARTS + LAG):
+        if part < PARTS:
+            rotate(part)
+        if part == 0:
+            send_evals.wait()
+            both = pair_evals[0] + pair_evals[1]
+            divisor = both[0:1, :] + 0.1 * both[1:2, :] / WIDTH
+        if part >= LAG:
+            send_back(part - LAG)
     for dz, dx in others:
         target = peer(dz, dx) * CORES + core
         remote(codes, all_codes.at[chip], codes_sem.at[0], codes_sem.at[1], layer, target).start()
-    send_pair.wait()
-    both = pair_send[...] + pair_recv[...]
-    damping = 0.1 * both[QUERIES + 1 : QUERIES + 2, :] / WIDTH
-    damped = (both[0:QUERIES, :] / (both[QUERIES : QUERIES + 1, :] + damping)).astype(BF16)
-
-    for dz, dx in others:
-        target = peer(dz, dx)
-        back_send[target] = dot(damped, basis[target], 1, 1).astype(BF16)
-        remote(
-            back_send.at[target], back_recv.at[chip], back_sem.at[0], back_sem.at[1 + dz], layer, target * CORES + core
-        ).start()
-    precond_sum = dot(damped, basis[chip], 1, 1)
-    back_recv[chip] = jnp.zeros((QUERIES, BLOCK), BF16)
 
     for sem in range(3):
         drain(train.at[:, pl.ds(0, ROWS), :], train_sem.at[sem])
@@ -192,25 +223,30 @@
         sorted_train[index, 0:ROWS, :] = dot(hit_0, train[index, 0:ROWS, :], 1, 0).astype(BF16)
         sorted_train[index, ROWS : 2 * ROWS, :] = dot(hit_1, train[index, ROWS : 2 * ROWS, :], 1, 0).astype(BF16)
 
-    for dz in (0, 1, 3, 2):
-        drain(back_recv.at[pl.ds(0, 3 if dz == 0 else 4)], back_sem.at[1 + dz])
-        precond_sum += jnp.sum(back_recv[pl.ds(row_of(dz) * SIDE, SIDE)].astype(F32), axis=0)
-    piece[...] = precond_sum.astype(BF16)
-    precond[z_hi, :, own_features] = piece[...]
-    for dz, dx in others:
-        target = peer(dz, dx) * CORES + core
-        remote(
-            piece, precond.at[z_hi, :, own_features], precond_sem.at[0], precond_sem.at[1 + dz], layer, target
-        ).start()
+    for part in range(PARTS):
+        precond_sum = own_parts[part]
+        for dz in (0, 1, 3, 2):
+            drain(back_recv.at[part, pl.ds(0, 3 if dz == 0 else 4)], back_sem.at[1 + part * SIDE + dz])
+            precond_sum += jnp.sum(back_recv[part, pl.ds(row_of(dz) * SIDE, SIDE)].astype(F32), axis=0)
+        piece[part] = precond_sum.astype(BF16)
+        precond[z_hi, pl.ds(part * PART, PART), own_features] = piece[part]
+        for dz, dx in others:
+            target = peer(dz, dx) * CORES + core
+            remote(
+                piece.at[part], precond.at[z_hi, pl.ds(part * PART, PART), own_features],
+                precond_sem.at[0], precond_sem.at[1 + part * SIDE + dz], layer, target,
+            ).start()
 
     total_scores = jnp.zeros((ROWS, BLOCK), F32)
     nothing = jnp.zeros((QUERIES, SIDE * BLOCK), BF16)
     for dz in (0, 1, 3, 2):
         row = row_of(dz)
-        if dz == 0:
-            drain(precond.at[0, :, pl.ds(0, 3 * BLOCK)], precond_sem.at[1])
-        else:
-            drain(precond.at[0], precond_sem.at[1 + dz])
+        for part in range(PARTS):
+            arrival = precond_sem.at[1 + part * SIDE + dz]
+            if dz == 0:
+                drain(precond.at[0, pl.ds(0, PART), pl.ds(0, 3 * BLOCK)], arrival)
+            else:
+                drain(precond.at[0, pl.ds(0, PART)], arrival)
         queries = precond[row]
         total_scores += dot(sorted_train[row, 0:ROWS, :], jnp.concatenate([queries, nothing], axis=0), 1, 1)
         total_scores += dot(sorted_train[row, ROWS : 2 * ROWS, :], jnp.concatenate([nothing, queries], axis=0), 1, 1)
@@ -268,10 +304,11 @@
     out_ref[...] = placed_0[0:QUERIES, :] + placed_1[QUERIES : 2 * QUERIES, :]
 
     for _ in range(5):
-        drain(gathered.at[0, :, pl.ds(0, 3 * BLOCK)], gather_sem.at[0])
+        drain(gathered.at[:, 0, :, pl.ds(0, 3 * BLOCK)], gather_sem.at[0])
+    drain(pair_send, pair_sem.at[0])
     drain(all_evals.at[pl.ds(0, 15)], evals_sem.at[0])
     drain(all_codes.at[pl.ds(0, 15)], codes_sem.at[0])
-    drain(back_recv.at[pl.ds(0, 15)], back_sem.at[0])
+    drain(back_recv.at[:, pl.ds(0, 15)], back_sem.at[0])
     for _ in range(5):
         drain(precond.at[0, :, pl.ds(0, 3 * BLOCK)], precond_sem.at[0])
     drain(layer_recv.at[pl.ds(0, 31)], layer_sem.at[0])
@@ -296,16 +333,17 @@
             pltpu.VMEM((CHIPS, BLOCK, CORES * BLOCK), BF16),
             pltpu.VMEM((SIDE, CORES * ROWS, SIDE * BLOCK), BF16),
             pltpu.VMEM((SIDE, CORES * ROWS, SIDE * BLOCK), BF16),
-            pltpu.VMEM((SIDE, QUERIES, SIDE * BLOCK), BF16),
-            pltpu.VMEM((QUERIES, BLOCK), BF16),
+            pltpu.VMEM((PARTS, SIDE, PART, SIDE * BLOCK), BF16),
+            pltpu.VMEM((PARTS, PART, BLOCK), BF16),
             pltpu.VMEM((CHIPS, 1, BLOCK), F32),
-            pltpu.VMEM((QUERIES + 8, CORES * BLOCK), F32),
-            pltpu.VMEM((QUERIES + 8, CORES * BLOCK), F32),
+            pltpu.VMEM((2, 8, CORES * BLOCK), F32),
+            pltpu.VMEM((PARTS, PART, CORES * BLOCK), F32),
+            pltpu.VMEM((PARTS, PART, CORES * BLOCK), F32),
             pltpu.VMEM((CORES, 1, ROWS), jnp.int32),
             pltpu.VMEM((CHIPS, CORES, 1, ROWS), jnp.int32),
-            pltpu.VMEM((CHIPS, QUERIES, BLOCK), BF16),
-            pltpu.VMEM((CHIPS, QUERIES, BLOCK), BF16),
-            pltpu.VMEM((QUERIES, BLOCK), BF16),
+            pltpu.VMEM((PARTS, SIDE, PART, SIDE * BLOCK), BF16),
+            pltpu.VMEM((PARTS, CHIPS, PART, BLOCK), BF16),
+            pltpu.VMEM((PARTS, PART, BLOCK), BF16),
             pltpu.VMEM((SIDE, QUERIES, SIDE * BLOCK), BF16),
             pltpu.VMEM((ROWS, BLOCK), F32),
             pltpu.VMEM((CORES * LAYERS, 8, BLOCK), F32),
@@ -315,12 +353,12 @@
             pltpu.SemaphoreType.DMA((2,)),
             pltpu.SemaphoreType.DMA((3,)),
             pltpu.SemaphoreType.DMA((2,)),
-            pltpu.SemaphoreType.DMA((5,)),
+            pltpu.SemaphoreType.DMA((1 + PARTS * SIDE,)),
+            pltpu.SemaphoreType.DMA((4,)),
+            pltpu.SemaphoreType.DMA((1 + PARTS,)),
             pltpu.SemaphoreType.DMA((2,)),
-            pltpu.SemaphoreType.DMA((2,)),
-            pltpu.SemaphoreType.DMA((2,)),
-            pltpu.SemaphoreType.DMA((5,)),
-            pltpu.SemaphoreType.DMA((5,)),
+            pltpu.SemaphoreType.DMA((1 + PARTS * SIDE,)),
+            pltpu.SemaphoreType.DMA((1 + PARTS * SIDE,)),
             pltpu.SemaphoreType.DMA((2,)),
             pltpu.SemaphoreType.DMA((3,)),
         ],

time: 58.6 us -> 55.3 us (0.944)
  Pallas kernels: 57.7 us -> 54.4 us
    pallas_call x1, Pallas kernels: 57.7 us -> 54.4 us  [on_device(): pl.pallas_call(kernel, out_shape=jax.ShapeDtypeStruct((QUERIES, ROWS), F3...]
where the time goes in v3:
time: 55.3 us; the launch traced here: 55 us
  Pallas kernels  54.4 us (98%)
  local copies, waits for them, and re-layouts  0.63 us (1%)
    pallas_call x1, Pallas kernels, on_device(): pl.pallas_call(kernel, out_shape=jax.ShapeDtypeStruct((QUERIES, ROWS), F3...  54.4 us

profile of v3, /device:TPU:1, one launch (start us, length us, event | category | flops | bytes accessed | tf_op | source)
XLA Modules:
  0.0 55.0 jit_solution(17859830069416681921)
XLA Ops:
  0.0 54.4 %shard_map.64 = f32[64,256]{1,0:T(8,128)S(1)} custom-call(bf16[1,256,128]{2,1,0:T(8,128)(2,1)} %pool_hbm.1, s32[1,64]{1,0:T(1,128)} %bitcast.5, bf16[1,16,2,128,128]{4,3,2,1,0:T(8,128)(2,1)} %bitcast.3, f32[1,128]{1,0:T(1,128)} %evals_hbm.1, bf16[1,256,4096]{2,1,0:T(8,128)(2,1)} %train_hbm.1, s32[1,256]{1,0:T(1,128)} %bitcast.4), custom_call_target="tpu_custom_call" | custom-call | flops 600000000 | bytes 4000000 | tf_op jit(solution)/shard_map/pallas_call | solution.py:323
  54.4 0.6 %copy.8 = f32[64,256]{1,0:T(8,128)} copy(f32[64,256]{1,0:T(8,128)S(1)} %shard_map.64) | data formatting | bytes 131072

commit v4 on v3

--- a/solution.py
+++ b/solution.py
@@ -7,8 +7,7 @@
 
 WIDTH = 4096
 QUERIES = 64
-PARTS = 2
-PART = QUERIES // PARTS
+PARTS = ((0, 32), (32, 32))
 LAG = 0
 LAYERS = 16
 CHIPS = 16
@@ -108,9 +107,9 @@
     for copy in small:
         copy.wait()
     pick = (lax.broadcasted_iota(jnp.int32, (256, QUERIES), 0) == qids[...]).astype(F32).astype(BF16)
-    message[...] = dot(pick, pool[...], 0, 0).astype(BF16).reshape(PARTS, PART, BLOCK)
+    message[...] = dot(pick, pool[...], 0, 0).astype(BF16)
     own_features = pl.ds(pl.multiple_of(x * BLOCK, BLOCK), BLOCK)
-    gathered[:, z_hi, :, own_features] = message[...]
+    gathered[z_hi, :, own_features] = message[...]
     all_evals[chip] = evals[...]
 
     pl.semaphore_wait(barrier, 15 + 31)
@@ -122,23 +121,16 @@
         eigen_hbm.at[0, :, 1 - core], basis.at[:, :, own_columns], basis_sem.at[0], basis_sem.at[1], layer, twin
     )
     send_basis.start()
-    for part in range(PARTS):
+    for part, (first, count) in enumerate(PARTS):
+        rows = pl.ds(first, count)
         for dz, dx in others:
             target = peer(dz, dx) * CORES + core
             remote(
-                message.at[part], gathered.at[part, z_hi, :, own_features],
+                message.at[rows], gathered.at[z_hi, rows, own_features],
                 gather_sem.at[0], gather_sem.at[1 + part * SIDE + dz], layer, target,
             ).start()
     send_ids = remote(ids.at[core], ids.at[core], ids_sem.at[0], ids_sem.at[1], layer, twin)
     send_ids.start()
-    for index in range(CHIPS):
-        sent = pl.ds(pl.multiple_of((index * CORES + 1 - core) * BLOCK, BLOCK), BLOCK)
-        to_columns = pl.ds((index % SIDE) * BLOCK, BLOCK)
-        remote(
-            train_hbm.at[0, :, sent], train.at[index // SIDE, own_rows, to_columns],
-            train_sem.at[1], train_sem.at[2], layer, twin,
-        ).start()
-
     send_ids.wait()
     hit_0, codes_0 = owner_order(ids[0])
     hit_1, codes_1 = owner_order(ids[1])
@@ -169,43 +161,47 @@
     own_parts = []
 
     def rotate(part):
-        rotated = jnp.zeros((PART, CORES * BLOCK), F32)
+        first, count = PARTS[part]
+        rotated = jnp.zeros((count, CORES * BLOCK), F32)
         for dz in (0, 1, 3, 2):
             row = row_of(dz)
             arrival = gather_sem.at[1 + part * SIDE + dz]
             if dz == 0:
-                drain(gathered.at[part, 0, :, pl.ds(0, 3 * BLOCK)], arrival)
+                drain(gathered.at[0, pl.ds(0, count), pl.ds(0, 3 * BLOCK)], arrival)
             else:
-                drain(gathered.at[part, 0], arrival)
-            rows = basis[pl.ds(row * SIDE, SIDE)].reshape(SIDE * BLOCK, CORES * BLOCK)
-            rotated += dot(gathered[part, row], rows, 1, 0)
-        pair_send[part] = rotated
+                drain(gathered.at[0, pl.ds(0, count)], arrival)
+            vectors = basis[pl.ds(row * SIDE, SIDE)].reshape(SIDE * BLOCK, CORES * BLOCK)
+            rotated += dot(gathered[row, first : first + count, :], vectors, 1, 0)
+        rows = pl.ds(first, count)
+        pair_send[first : first + count, :] = rotated
         send_pair.append(
-            remote(pair_send.at[part], pair_recv.at[part], pair_sem.at[0], pair_sem.at[1 + part], layer, twin)
+            remote(pair_send.at[rows], pair_recv.at[rows], pair_sem.at[0], pair_sem.at[1 + part], layer, twin)
         )
         send_pair[part].start()
 
     def send_back(part):
+        first, count = PARTS[part]
+        rows = pl.ds(first, count)
         send_pair[part].wait_recv()
-        damped = ((pair_send[part] + pair_recv[part]) / divisor).astype(BF16)
+        damped = ((pair_send[first : first + count, :] + pair_recv[first : first + count, :]) / divisor).astype(BF16)
         for dz in (2, 1, 3, 0):
             row = lax.rem(z_hi + dz, SIDE)
-            rows = basis[pl.ds(row * SIDE, SIDE)].reshape(SIDE * BLOCK, CORES * BLOCK)
-            back_send[part, row] = dot(damped, rows, 1, 1).astype(BF16)
+            vectors = basis[pl.ds(row * SIDE, SIDE)].reshape(SIDE * BLOCK, CORES * BLOCK)
+            back_send[row, first : first + count, :] = dot(damped, vectors, 1, 1).astype(BF16)
             for dx in (2, 1, 3, 0):
                 if dz == 0 and dx == 0:
                     continue
                 column = lax.rem(x + dx, SIDE)
                 block = pl.ds(pl.multiple_of(column * BLOCK, BLOCK), BLOCK)
                 remote(
-                    back_send.at[part, row, :, block], back_recv.at[part, chip],
+                    back_send.at[row, rows, block], back_recv.at[chip, rows],
                     back_sem.at[0], back_sem.at[1 + part * SIDE + dz], layer, (row * SIDE + column) * CORES + core,
                 ).start()
         own_parts.append(dot(damped, basis[chip], 1, 1))
-        back_recv[part, chip] = jnp.zeros((PART, BLOCK), BF16)
-
-    for part in range(PARTS + LAG):
-        if part < PARTS:
+        back_recv[chip, first : first + count, :] = jnp.zeros((count, BLOCK), BF16)
+
+    for part in range(len(PARTS) + LAG):
+        if part < len(PARTS):
             rotate(part)
         if part == 0:
             send_evals.wait()
@@ -213,9 +209,14 @@
             divisor = both[0:1, :] + 0.1 * both[1:2, :] / WIDTH
         if part >= LAG:
             send_back(part - LAG)
-    for dz, dx in others:
-        target = peer(dz, dx) * CORES + core
-        remote(codes, all_codes.at[chip], codes_sem.at[0], codes_sem.at[1], layer, target).start()
+
+    for index in range(CHIPS):
+        sent = pl.ds(pl.multiple_of((index * CORES + 1 - core) * BLOCK, BLOCK), BLOCK)
+        to_columns = pl.ds((index % SIDE) * BLOCK, BLOCK)
+        remote(
+            train_hbm.at[0, :, sent], train.at[index // SIDE, own_rows, to_columns],
+            train_sem.at[1], train_sem.at[2], layer, twin,
+        ).start()
 
     for sem in range(3):
         drain(train.at[:, pl.ds(0, ROWS), :], train_sem.at[sem])
@@ -223,34 +224,34 @@
         sorted_train[index, 0:ROWS, :] = dot(hit_0, train[index, 0:ROWS, :], 1, 0).astype(BF16)
         sorted_train[index, ROWS : 2 * ROWS, :] = dot(hit_1, train[index, ROWS : 2 * ROWS, :], 1, 0).astype(BF16)
 
-    for part in range(PARTS):
+    for part, (first, count) in enumerate(PARTS):
+        rows = pl.ds(first, count)
         precond_sum = own_parts[part]
         for dz in (0, 1, 3, 2):
-            drain(back_recv.at[part, pl.ds(0, 3 if dz == 0 else 4)], back_sem.at[1 + part * SIDE + dz])
-            precond_sum += jnp.sum(back_recv[part, pl.ds(row_of(dz) * SIDE, SIDE)].astype(F32), axis=0)
-        piece[part] = precond_sum.astype(BF16)
-        precond[z_hi, pl.ds(part * PART, PART), own_features] = piece[part]
+            drain(back_recv.at[pl.ds(0, 3 if dz == 0 else 4), pl.ds(0, count)], back_sem.at[1 + part * SIDE + dz])
+            arrived = back_recv[pl.ds(row_of(dz) * SIDE, SIDE), first : first + count, :]
+            precond_sum += jnp.sum(arrived.astype(F32), axis=0)
+        piece[first : first + count, :] = precond_sum.astype(BF16)
+        precond[z_hi, first : first + count, own_features] = piece[first : first + count, :]
         for dz, dx in others:
             target = peer(dz, dx) * CORES + core
             remote(
-                piece.at[part], precond.at[z_hi, pl.ds(part * PART, PART), own_features],
+                piece.at[rows], precond.at[z_hi, rows, own_features],
                 precond_sem.at[0], precond_sem.at[1 + part * SIDE + dz], layer, target,
             ).start()
 
-    total_scores = jnp.zeros((ROWS, BLOCK), F32)
-    nothing = jnp.zeros((QUERIES, SIDE * BLOCK), BF16)
+    by_query = jnp.zeros((QUERIES, CORES * ROWS), F32)
     for dz in (0, 1, 3, 2):
         row = row_of(dz)
-        for part in range(PARTS):
+        for part, (first, count) in enumerate(PARTS):
             arrival = precond_sem.at[1 + part * SIDE + dz]
             if dz == 0:
-                drain(precond.at[0, pl.ds(0, PART), pl.ds(0, 3 * BLOCK)], arrival)
+                drain(precond.at[0, pl.ds(0, count), pl.ds(0, 3 * BLOCK)], arrival)
             else:
-                drain(precond.at[0, pl.ds(0, PART)], arrival)
-        queries = precond[row]
-        total_scores += dot(sorted_train[row, 0:ROWS, :], jnp.concatenate([queries, nothing], axis=0), 1, 1)
-        total_scores += dot(sorted_train[row, ROWS : 2 * ROWS, :], jnp.concatenate([nothing, queries], axis=0), 1, 1)
-    scores[...] = total_scores
+                drain(precond.at[0, pl.ds(0, count)], arrival)
+        by_query += dot(precond[row], sorted_train[row], 1, 1)
+    by_core = jnp.concatenate([by_query[:, 0:ROWS], by_query[:, ROWS : 2 * ROWS]], axis=0)
+    scores[...] = by_core.T
     mine_at = layer * CORES + core
     for step in LAYER_STEPS:
         other = lax.rem(layer + step, LAYERS)
@@ -263,7 +264,28 @@
                 scores.at[rows, :], layer_recv.at[mine_at], layer_sem.at[0], layer_sem.at[1],
                 other, chip * CORES + to_core,
             ).start()
+    for dz, dx in others:
+        target = peer(dz, dx) * CORES + core
+        remote(codes, all_codes.at[chip], codes_sem.at[0], codes_sem.at[1], layer, target).start()
     layer_recv[mine_at] = scores[pl.ds(pl.multiple_of(mine_at * 8, 8), 8), :]
+
+    drain(layer_recv.at[pl.ds(0, 31)], layer_sem.at[1])
+    tile[...] = jnp.sum(layer_recv[...], axis=0)
+
+    owner = layer * CORES + core
+    for step in LAYER_STEPS:
+        if step == 0:
+            continue
+        other = lax.rem(layer + step, LAYERS)
+        remote(tile, final.at[chip], final_sem.at[0], final_sem.at[1], other, owner).start()
+
+    @pl.when(layer != chip)
+    def _():
+        remote(tile, final.at[chip], final_sem.at[2], final_sem.at[1], layer, owner).start()
+
+    @pl.when(layer == chip)
+    def _():
+        pltpu.make_async_copy(tile, final.at[chip], final_sem.at[1]).start()
 
     drain(all_codes.at[pl.ds(0, 15)], codes_sem.at[1])
     rank = lax.broadcasted_iota(jnp.int32, (CHIPS, 8, ROWS), 1)
@@ -275,40 +297,21 @@
         slot = (code - place * ROWS).astype(F32)
         wanted = jnp.sum(jnp.where(place - 8 * blk == rank, slot, 0.0), axis=2, keepdims=True)
         put.append((wanted == lane).astype(F32).reshape(BLOCK, ROWS).astype(BF16))
-
-    drain(layer_recv.at[pl.ds(0, 31)], layer_sem.at[1])
-    tile[...] = jnp.sum(layer_recv[...], axis=0)
-
-    owner = layer * CORES + core
-    for step in LAYER_STEPS:
-        if step == 0:
-            continue
-        other = lax.rem(layer + step, LAYERS)
-        remote(tile, final.at[chip], final_sem.at[0], final_sem.at[1], other, owner).start()
-
-    @pl.when(layer != chip)
-    def _():
-        remote(tile, final.at[chip], final_sem.at[2], final_sem.at[1], layer, owner).start()
-
-    @pl.when(layer == chip)
-    def _():
-        pltpu.make_async_copy(tile, final.at[chip], final_sem.at[1]).start()
+    put = jnp.concatenate(put, axis=0)
 
     drain(final, final_sem.at[1])
-    values = final[...].reshape(BLOCK, BLOCK)
-    placed_0 = jnp.zeros((BLOCK, ROWS), F32)
-    placed_1 = jnp.zeros((BLOCK, ROWS), F32)
-    for term in split3(values):
-        placed_0 += dot(term, put[0], 0, 0)
-        placed_1 += dot(term, put[1], 0, 0)
-    out_ref[...] = placed_0[0:QUERIES, :] + placed_1[QUERIES : 2 * QUERIES, :]
+    values = final[...].reshape(BLOCK, BLOCK).T
+    values = jnp.concatenate([values[0:QUERIES, :], values[QUERIES : 2 * QUERIES, :]], axis=1)
+    placed = dot(jnp.concatenate(split3(values), axis=0), put, 1, 0)
+    placed = placed[0:QUERIES, :] + placed[QUERIES : 2 * QUERIES, :] + placed[2 * QUERIES : 3 * QUERIES, :]
+    out_ref[...] = placed
 
     for _ in range(5):
-        drain(gathered.at[:, 0, :, pl.ds(0, 3 * BLOCK)], gather_sem.at[0])
+        drain(gathered.at[0, :, pl.ds(0, 3 * BLOCK)], gather_sem.at[0])
     drain(pair_send, pair_sem.at[0])
     drain(all_evals.at[pl.ds(0, 15)], evals_sem.at[0])
     drain(all_codes.at[pl.ds(0, 15)], codes_sem.at[0])
-    drain(back_recv.at[:, pl.ds(0, 15)], back_sem.at[0])
+    drain(back_recv.at[pl.ds(0, 15)], back_sem.at[0])
     for _ in range(5):
         drain(precond.at[0, :, pl.ds(0, 3 * BLOCK)], precond_sem.at[0])
     drain(layer_recv.at[pl.ds(0, 31)], layer_sem.at[0])
@@ -333,17 +336,17 @@
             pltpu.VMEM((CHIPS, BLOCK, CORES * BLOCK), BF16),
             pltpu.VMEM((SIDE, CORES * ROWS, SIDE * BLOCK), BF16),
             pltpu.VMEM((SIDE, CORES * ROWS, SIDE * BLOCK), BF16),
-            pltpu.VMEM((PARTS, SIDE, PART, SIDE * BLOCK), BF16),
-            pltpu.VMEM((PARTS, PART, BLOCK), BF16),
+            pltpu.VMEM((SIDE, QUERIES, SIDE * BLOCK), BF16),
+            pltpu.VMEM((QUERIES, BLOCK), BF16),
             pltpu.VMEM((CHIPS, 1, BLOCK), F32),
             pltpu.VMEM((2, 8, CORES * BLOCK), F32),
-            pltpu.VMEM((PARTS, PART, CORES * BLOCK), F32),
-            pltpu.VMEM((PARTS, PART, CORES * BLOCK), F32),
+            pltpu.VMEM((QUERIES, CORES * BLOCK), F32),
+            pltpu.VMEM((QUERIES, CORES * BLOCK), F32),
             pltpu.VMEM((CORES, 1, ROWS), jnp.int32),
             pltpu.VMEM((CHIPS, CORES, 1, ROWS), jnp.int32),
-            pltpu.VMEM((PARTS, SIDE, PART, SIDE * BLOCK), BF16),
-            pltpu.VMEM((PARTS, CHIPS, PART, BLOCK), BF16),
-            pltpu.VMEM((PARTS, PART, BLOCK), BF16),
+            pltpu.VMEM((SIDE, QUERIES, SIDE * BLOCK), BF16),
+            pltpu.VMEM((CHIPS, QUERIES, BLOCK), BF16),
+            pltpu.VMEM((QUERIES, BLOCK), BF16),
             pltpu.VMEM((SIDE, QUERIES, SIDE * BLOCK), BF16),
             pltpu.VMEM((ROWS, BLOCK), F32),
             pltpu.VMEM((CORES * LAYERS, 8, BLOCK), F32),
@@ -353,12 +356,12 @@
             pltpu.SemaphoreType.DMA((2,)),
             pltpu.SemaphoreType.DMA((3,)),
             pltpu.SemaphoreType.DMA((2,)),
-            pltpu.SemaphoreType.DMA((1 + PARTS * SIDE,)),
+            pltpu.SemaphoreType.DMA((1 + len(PARTS) * SIDE,)),
             pltpu.SemaphoreType.DMA((4,)),
-            pltpu.SemaphoreType.DMA((1 + PARTS,)),
+            pltpu.SemaphoreType.DMA((1 + len(PARTS),)),
             pltpu.SemaphoreType.DMA((2,)),
-            pltpu.SemaphoreType.DMA((1 + PARTS * SIDE,)),
-            pltpu.SemaphoreType.DMA((1 + PARTS * SIDE,)),
+            pltpu.SemaphoreType.DMA((1 + len(PARTS) * SIDE,)),
+            pltpu.SemaphoreType.DMA((1 + len(PARTS) * SIDE,)),
             pltpu.SemaphoreType.DMA((2,)),
             pltpu.SemaphoreType.DMA((3,)),
         ],

time: 55.3 us -> 54.7 us (0.989)
  no operation moved by 1% of the time
where the time goes in v4:
time: 54.7 us; the launch traced here: 54.5 us
  Pallas kernels  53.9 us (99%)
  local copies, waits for them, and re-layouts  0.63 us (1%)
    pallas_call x1, Pallas kernels, on_device(): pl.pallas_call(kernel, out_shape=jax.ShapeDtypeStruct((QUERIES, ROWS), F3...  53.9 us

profile of v4, /device:TPU:1, one launch (start us, length us, event | category | flops | bytes accessed | tf_op | source)
XLA Modules:
  0.0 54.5 jit_solution(11008902305630611325)
XLA Ops:
  0.0 53.9 %shard_map.64 = f32[64,256]{1,0:T(8,128)S(1)} custom-call(bf16[1,256,128]{2,1,0:T(8,128)(2,1)} %pool_hbm.1, s32[1,64]{1,0:T(1,128)} %bitcast.5, bf16[1,16,2,128,128]{4,3,2,1,0:T(8,128)(2,1)} %bitcast.3, f32[1,128]{1,0:T(1,128)} %evals_hbm.1, bf16[1,256,4096]{2,1,0:T(8,128)(2,1)} %train_hbm.1, s32[1,256]{1,0:T(1,128)} %bitcast.4), custom_call_target="tpu_custom_call" | custom-call | flops 600000000 | bytes 4000000 | tf_op jit(solution)/shard_map/pallas_call | solution.py:326
  53.9 0.6 %copy.8 = f32[64,256]{1,0:T(8,128)} copy(f32[64,256]{1,0:T(8,128)S(1)} %shard_map.64) | data formatting | bytes 131072

commit v5 on v4

--- a/solution.py
+++ b/solution.py
@@ -79,11 +79,10 @@
     barrier = pltpu.get_barrier_semaphore()
     for dz, dx in others:
         pl.semaphore_signal(barrier, inc=1, device_id=(layer, peer(dz, dx) * CORES + core), device_id_type=MESH)
-    for step in range(LAYERS):
+    pl.semaphore_signal(barrier, inc=1, device_id=(layer, twin), device_id_type=MESH)
+    for step in range(1, LAYERS):
         other = lax.rem(layer + step, LAYERS)
-        if step > 0:
-            pl.semaphore_signal(barrier, inc=1, device_id=(other, blk), device_id_type=MESH)
-        pl.semaphore_signal(barrier, inc=1, device_id=(other, twin), device_id_type=MESH)
+        pl.semaphore_signal(barrier, inc=1, device_id=(other, blk), device_id_type=MESH)
 
     small = [
         pltpu.make_async_copy(pool_hbm.at[0], pool, local_sem.at[0]),
@@ -97,13 +96,6 @@
     own_basis = pltpu.make_async_copy(eigen_hbm.at[0, :, core], basis.at[:, :, own_columns], local_sem.at[4])
     own_basis.start()
     own_rows = pl.ds(pl.multiple_of(core * ROWS, ROWS), ROWS)
-    for index in range(CHIPS):
-        kept = pl.ds(pl.multiple_of((index * CORES + core) * BLOCK, BLOCK), BLOCK)
-        to_columns = pl.ds((index % SIDE) * BLOCK, BLOCK)
-        pltpu.make_async_copy(
-            train_hbm.at[0, :, kept], train.at[index // SIDE, own_rows, to_columns], train_sem.at[0]
-        ).start()
-
     for copy in small:
         copy.wait()
     pick = (lax.broadcasted_iota(jnp.int32, (256, QUERIES), 0) == qids[...]).astype(F32).astype(BF16)
@@ -112,7 +104,7 @@
     gathered[z_hi, :, own_features] = message[...]
     all_evals[chip] = evals[...]
 
-    pl.semaphore_wait(barrier, 15 + 31)
+    pl.semaphore_wait(barrier, 15 + 1 + 15)
 
     for dz, dx in others:
         target = peer(dz, dx) * CORES + core
@@ -131,6 +123,13 @@
             ).start()
     send_ids = remote(ids.at[core], ids.at[core], ids_sem.at[0], ids_sem.at[1], layer, twin)
     send_ids.start()
+    for index in range(CHIPS):
+        kept = pl.ds(pl.multiple_of((index * CORES + core) * BLOCK, BLOCK), BLOCK)
+        to_columns = pl.ds((index % SIDE) * BLOCK, BLOCK)
+        pltpu.make_async_copy(
+            train_hbm.at[0, :, kept], train.at[index // SIDE, own_rows, to_columns], train_sem.at[0]
+        ).start()
+
     send_ids.wait()
     hit_0, codes_0 = owner_order(ids[0])
     hit_1, codes_1 = owner_order(ids[1])

time: 54.7 us -> 54.7 us (level)
  no operation moved by 1% of the time
where the time goes in v5:
time: 54.7 us; the launch traced here: 54.5 us
  Pallas kernels  53.9 us (99%)
  local copies, waits for them, and re-layouts  0.63 us (1%)
    pallas_call x1, Pallas kernels, on_device(): pl.pallas_call(kernel, out_shape=jax.ShapeDtypeStruct((QUERIES, ROWS), F3...  53.9 us

profile of v5, /device:TPU:1, one launch (start us, length us, event | category | flops | bytes accessed | tf_op | source)
XLA Modules:
  0.0 54.5 jit_solution(5779647936167919553)
XLA Ops:
  0.0 53.9 %shard_map.64 = f32[64,256]{1,0:T(8,128)S(1)} custom-call(bf16[1,256,128]{2,1,0:T(8,128)(2,1)} %pool_hbm.1, s32[1,64]{1,0:T(1,128)} %bitcast.5, bf16[1,16,2,128,128]{4,3,2,1,0:T(8,128)(2,1)} %bitcast.3, f32[1,128]{1,0:T(1,128)} %evals_hbm.1, bf16[1,256,4096]{2,1,0:T(8,128)(2,1)} %train_hbm.1, s32[1,256]{1,0:T(1,128)} %bitcast.4), custom_call_target="tpu_custom_call" | custom-call | flops 600000000 | bytes 4000000 | tf_op jit(solution)/shard_map/pallas_call | solution.py:325
  53.9 0.6 %copy.8 = f32[64,256]{1,0:T(8,128)} copy(f32[64,256]{1,0:T(8,128)S(1)} %shard_map.64) | data formatting | bytes 131072
